TPU v7x, 32 devices: a whole 2x2x4 slice. The times are simulated.
32 devices in a mesh: prompt: 4 (over y, x), tensor: 8 (over z, core).
Axes of the slice: x: 2, y: 2, z: 4, core: 2. Of those that a mesh axis runs over, the one named last changes fastest.
Arguments:
- tokens: bfloat16 [4, 128, 8192], P('prompt')
- gate_weight: bfloat16 [8192, 28672], P('prompt', 'tensor'), may hold values from -0.0625 to 0.0625
- up_weight: bfloat16 [8192, 28672], P('prompt', 'tensor'), may hold values from -0.0625 to 0.0625
- down_weight: bfloat16 [28672, 8192], P('tensor', 'prompt')
- norm_gain: float32 [8192], P('prompt'), may hold values from 0.1 to 1.9
- unembed: bfloat16 [8192, 86016], P('prompt', 'tensor'), may hold values from -0.5 to 0.5
- guidance: float32 [4], replicated, may hold values from -1.5 to 2.5
- logit_bias: float32 [128, 86016], P('prompt', 'tensor'), may hold values from -2 to 322
Outputs:
- log_probs: float32 [128, 86016], P('prompt', 'tensor')
All inputs are finite; a program needn't handle non-finite values.
Results may differ from a plain program's by a relative error of at most 0.0025.
Values may be sent and summed in bfloat16 or wider, within the bound.
A program may use at most 192 MiB of HBM per device.

v0:
```python
import functools

import jax
import jax.numpy as jnp
from jax import lax
from jax.experimental import pallas as pl
from jax.experimental.pallas import tpu as pltpu
from jax.sharding import PartitionSpec as P

MESH = pl.DeviceIdType.MESH
F32 = jnp.float32
BF16 = jnp.bfloat16


def step_of(size, most):
    step = most
    while size % step:
        step //= 2
    return step


def greet(axes):
    barrier = pltpu.get_barrier_semaphore()
    count = 0
    for axis, n in axes:
        me = lax.axis_index(axis)
        for d in range(1, n):
            pl.semaphore_signal(barrier, inc=1, device_id={axis: lax.rem(me + d, n)}, device_id_type=MESH)
            count += 1
    pl.semaphore_wait(barrier, count)


def ffn_kernel(
    n, x_ref, gate_hbm, up_hbm, down_hbm, out_ref,
    wg, wu, wd, part, send, recv, own, hid, acc,
    w_sem, d_sem, ps_sem, pr_sem, hs_sem, hr_sem,
):
    me = lax.axis_index("prompt")
    rows, share = x_ref.shape[1:]
    steps, chunk = hid.shape[0], hid.shape[3]

    def weights(k, slot):
        at = pl.ds(pl.multiple_of(k * chunk, chunk), chunk)
        return (
            pltpu.make_async_copy(gate_hbm.at[:, at], wg.at[slot], w_sem.at[slot, 0]),
            pltpu.make_async_copy(up_hbm.at[:, at], wu.at[slot], w_sem.at[slot, 1]),
        )

    def down(k, slot):
        at = pl.ds(pl.multiple_of(k * chunk, chunk), chunk)
        return pltpu.make_async_copy(down_hbm.at[at, :], wd.at[slot], d_sem.at[slot])

    def send_part(k, d):
        q = lax.rem(me + d, n)
        return pltpu.make_async_remote_copy(
            src_ref=send.at[k, q], dst_ref=recv.at[k, d - 1],
            send_sem=ps_sem.at[k, d - 1], recv_sem=pr_sem.at[k, d - 1],
            device_id={"prompt": q}, device_id_type=MESH,
        )

    def send_hid(k, d, owner):
        q = lax.rem(me + d, n)
        return pltpu.make_async_remote_copy(
            src_ref=hid.at[k, owner], dst_ref=hid.at[k, owner],
            send_sem=hs_sem.at[k, d - 1], recv_sem=hr_sem.at[k, d - 1],
            device_id={"prompt": q}, device_id_type=MESH,
        )

    for copy in weights(0, 0):
        copy.start()
    down(0, 0).start()
    greet([("prompt", n)])

    @pl.loop(0, steps)
    def _(k):
        slot = lax.rem(k, 2)
        for copy in weights(k, slot):
            copy.wait()

        @pl.when(k + 1 < steps)
        def _():
            for copy in weights(k + 1, 1 - slot):
                copy.start()

        x = x_ref[...].reshape(n * rows, share)
        part[:, :, :chunk] = jnp.dot(x, wg[slot], preferred_element_type=F32).reshape(n, rows, chunk)
        part[:, :, chunk:] = jnp.dot(x, wu[slot], preferred_element_type=F32).reshape(n, rows, chunk)
        send[k] = part[...].astype(BF16)
        own[k] = part[me]
        for d in range(1, n):
            send_part(k, d).start()

    @pl.loop(0, steps)
    def _(k):
        for d in range(1, n):
            send_part(k, d).wait_recv()
        total = own[k]
        for d in range(1, n):
            total = total + recv[k, d - 1].astype(F32)
        gate = total[:, :chunk]
        hid[k, me] = (gate / (1.0 + jnp.exp(-gate)) * total[:, chunk:]).astype(BF16)
        for d in range(1, n):
            send_hid(k, d, me).start()

    acc[...] = jnp.zeros_like(acc)
    tile = step_of(share, 512)

    @pl.loop(0, steps)
    def _(k):
        slot = lax.rem(k, 2)
        down(k, slot).wait()

        @pl.when(k + 1 < steps)
        def _():
            down(k + 1, 1 - slot).start()

        for d in range(1, n):
            send_hid(k, d, lax.rem(me + n - d, n)).wait_recv()
        h = hid[k].reshape(n * rows, chunk)
        for t in range(share // tile):
            at = slice(t * tile, (t + 1) * tile)
            acc[:, at] += jnp.dot(h, wd[slot, :, at], preferred_element_type=F32)

    out_ref[...] = acc[...].astype(BF16)

    @pl.loop(0, steps)
    def _(k):
        for d in range(1, n):
            send_part(k, d).wait_send()
            send_hid(k, d, me).wait_send()


def ffn(n, x, gate_weight, up_weight, down_weight):
    rows, share = x.shape[1:]
    width = gate_weight.shape[1]
    chunk = step_of(width, 256)
    steps = width // chunk
    dma = pltpu.SemaphoreType.DMA
    hbm = pl.BlockSpec(memory_space=pl.ANY)
    vmem = pl.BlockSpec(memory_space=pltpu.VMEM)
    return pl.pallas_call(
        functools.partial(ffn_kernel, n),
        out_shape=jax.ShapeDtypeStruct((n * rows, share), BF16),
        in_specs=[vmem, hbm, hbm, hbm],
        out_specs=vmem,
        scratch_shapes=[
            pltpu.VMEM((2, share, chunk), BF16),
            pltpu.VMEM((2, share, chunk), BF16),
            pltpu.VMEM((2, chunk, share), BF16),
            pltpu.VMEM((n, rows, 2 * chunk), F32),
            pltpu.VMEM((steps, n, rows, 2 * chunk), BF16),
            pltpu.VMEM((steps, n - 1, rows, 2 * chunk), BF16),
            pltpu.VMEM((steps, rows, 2 * chunk), F32),
            pltpu.VMEM((steps, n, rows, chunk), BF16),
            pltpu.VMEM((n * rows, share), F32),
            dma((2, 2)),
            dma((2,)),
            dma((steps, n - 1)),
            dma((steps, n - 1)),
            dma((steps, n - 1)),
            dma((steps, n - 1)),
        ],
        compiler_params=pltpu.CompilerParams(
            collective_id=0, has_side_effects=True, vmem_limit_bytes=56 * 1024 * 1024
        ),
        name="ffn",
    )(x, gate_weight, up_weight, down_weight)


def head_kernel(
    n, m, x_ref, unembed_hbm, bias_ref, out_ref,
    w, send, recv, own, mine, stats,
    w_sem, ps_sem, pr_sem, ss_sem, sr_sem,
):
    me = lax.axis_index("prompt")
    tp = lax.axis_index("tensor")
    steps, _, rows, chunk = send.shape
    slots = w.shape[0]

    def columns(k):
        return pl.ds(pl.multiple_of(k * chunk, chunk), chunk)

    def weights(k):
        slot = lax.rem(k, slots)
        return pltpu.make_async_copy(unembed_hbm.at[:, columns(k)], w.at[slot], w_sem.at[slot])

    def send_part(k, d):
        q = lax.rem(me + d, n)
        return pltpu.make_async_remote_copy(
            src_ref=send.at[k, q], dst_ref=recv.at[k, d - 1],
            send_sem=ps_sem.at[k, d - 1], recv_sem=pr_sem.at[k, d - 1],
            device_id={"prompt": q}, device_id_type=MESH,
        )

    def send_stats(d):
        return pltpu.make_async_remote_copy(
            src_ref=mine, dst_ref=stats.at[d - 1],
            send_sem=ss_sem.at[d - 1], recv_sem=sr_sem.at[d - 1],
            device_id={"tensor": lax.rem(tp + d, m)}, device_id_type=MESH,
        )

    for k in range(slots - 1):
        weights(k).start()
    greet([("prompt", n), ("tensor", m)])

    @pl.loop(0, steps)
    def _(k):
        weights(k).wait()

        @pl.when(k + slots - 1 < steps)
        def _():
            weights(k + slots - 1).start()

        product = jnp.dot(x_ref[...], w[lax.rem(k, slots)], preferred_element_type=F32)
        own[...] = product.reshape(n, rows, chunk)
        send[k] = own[...].astype(BF16)
        out_ref[:, columns(k)] = own[me]
        for d in range(1, n):
            send_part(k, d).start()

    def gather(k, top):
        for d in range(1, n):
            send_part(k, d).wait_recv()
        total = out_ref[:, columns(k)]
        for d in range(1, n):
            total = total + recv[k, d - 1].astype(F32)
        total = total + bias_ref[:, columns(k)]
        out_ref[:, columns(k)] = total
        return jnp.maximum(top, jnp.max(total, axis=1, keepdims=True))

    top = lax.fori_loop(0, steps, gather, jnp.full((rows, 1), -jnp.inf, F32))

    def expsum(k, total):
        return total + jnp.sum(jnp.exp(out_ref[:, columns(k)] - top), axis=1, keepdims=True)

    total = lax.fori_loop(0, steps, expsum, jnp.zeros((rows, 1), F32))
    mine[0] = jnp.broadcast_to(top, (rows, 128))
    mine[1] = jnp.broadcast_to(total, (rows, 128))
    for d in range(1, m):
        send_stats(d).start()
    best = mine[0]
    for d in range(1, m):
        send_stats(d).wait_recv()
        best = jnp.maximum(best, stats[d - 1, 0])
    grand = mine[1] * jnp.exp(mine[0] - best)
    for d in range(1, m):
        grand = grand + stats[d - 1, 1] * jnp.exp(stats[d - 1, 0] - best)
    shift = (best + jnp.log(grand))[:, :1]

    @pl.loop(0, steps)
    def _(k):
        out_ref[:, columns(k)] = out_ref[:, columns(k)] - shift
        for d in range(1, n):
            send_part(k, d).wait_send()

    for d in range(1, m):
        send_stats(d).wait_send()


def head(n, m, mixed, unembed, bias):
    share, width = unembed.shape
    rows = mixed.shape[0] // n
    chunk = step_of(width, 512)
    steps = width // chunk
    dma = pltpu.SemaphoreType.DMA
    hbm = pl.BlockSpec(memory_space=pl.ANY)
    vmem = pl.BlockSpec(memory_space=pltpu.VMEM)
    return pl.pallas_call(
        functools.partial(head_kernel, n, m),
        out_shape=jax.ShapeDtypeStruct((rows, width), F32),
        in_specs=[vmem, hbm, vmem],
        out_specs=vmem,
        scratch_shapes=[
            pltpu.VMEM((4, share, chunk), BF16),
            pltpu.VMEM((steps, n, rows, chunk), BF16),
            pltpu.VMEM((steps, n - 1, rows, chunk), BF16),
            pltpu.VMEM((n, rows, chunk), F32),
            pltpu.VMEM((2, rows, 128), F32),
            pltpu.VMEM((m - 1, 2, rows, 128), F32),
            dma((4,)),
            dma((steps, n - 1)),
            dma((steps, n - 1)),
            dma((m - 1,)),
            dma((m - 1,)),
        ],
        compiler_params=pltpu.CompilerParams(
            collective_id=1, has_side_effects=True, vmem_limit_bytes=48 * 1024 * 1024
        ),
        name="head",
    )(mixed, unembed, bias)


def mid_kernel(
    n, m, branch_ref, tokens_ref, gain_ref, guidance_ref, out_ref,
    pair, send, recv, state, sums, others,
    p_sem, s_sem, r_sem, qs_sem, qr_sem, os_sem, or_sem, f_sem,
):
    me = lax.axis_index("prompt")
    tp = lax.axis_index("tensor")
    chips = m // 2
    chip, core = tp // 2, lax.rem(tp, 2)
    share = gain_ref.shape[1]
    rows = state.shape[0]
    mine = rows // n

    def at_chip(d):
        return lax.rem(chip + d, chips)

    def to_pair(c):
        return pltpu.make_async_remote_copy(
            src_ref=branch_ref.at[2 * c + 1 - core], dst_ref=pair.at[c],
            send_sem=p_sem.at[0, c], recv_sem=p_sem.at[1, c],
            device_id={"tensor": 2 * chip + 1 - core}, device_id_type=MESH,
        )

    def to_chip(d):
        return pltpu.make_async_remote_copy(
            src_ref=send.at[d - 1], dst_ref=recv.at[d - 1],
            send_sem=s_sem.at[d - 1], recv_sem=r_sem.at[d - 1],
            device_id={"tensor": 2 * at_chip(d) + core}, device_id_type=MESH,
        )

    def to_group(d):
        return pltpu.make_async_remote_copy(
            src_ref=sums, dst_ref=others.at[d - 1],
            send_sem=qs_sem.at[d - 1], recv_sem=qr_sem.at[d - 1],
            device_id={"prompt": lax.rem(me + d, n)}, device_id_type=MESH,
        )

    def block_out(d, owner):
        return pltpu.make_async_remote_copy(
            src_ref=out_ref.at[owner], dst_ref=out_ref.at[owner],
            send_sem=os_sem.at[d - 1], recv_sem=or_sem.at[d - 1],
            device_id={"tensor": 2 * at_chip(d) + core}, device_id_type=MESH,
        )

    def pass_on(e, owner):
        return pltpu.make_async_remote_copy(
            src_ref=out_ref.at[owner], dst_ref=out_ref.at[owner],
            send_sem=f_sem.at[0, e], recv_sem=f_sem.at[1, e],
            device_id={"tensor": 2 * chip + 1 - core}, device_id_type=MESH,
        )

    barrier = pltpu.get_barrier_semaphore()
    pl.semaphore_signal(barrier, inc=1, device_id={"tensor": 2 * chip + 1 - core}, device_id_type=MESH)
    for d in range(1, chips):
        pl.semaphore_signal(barrier, inc=1, device_id={"tensor": 2 * at_chip(d) + core}, device_id_type=MESH)
    for d in range(1, n):
        pl.semaphore_signal(barrier, inc=1, device_id={"prompt": lax.rem(me + d, n)}, device_id_type=MESH)
    pl.semaphore_wait(barrier, 1 + chips - 1 + n - 1)

    order = list(range(1, chips)) + [0]
    for d in order:
        to_pair(at_chip(d)).start()
    for d in range(1, chips):
        c = at_chip(d)
        to_pair(c).wait_recv()
        send[d - 1] = (branch_ref[2 * c + core].astype(F32) + pair[c].astype(F32)).astype(BF16)
        to_chip(d).start()
    to_pair(chip).wait_recv()
    state[...] = (
        tokens_ref[tp].astype(F32) + branch_ref[tp].astype(F32) + pair[chip].astype(F32)
    )
    for d in range(1, chips):
        to_chip(d).wait_recv()
        state[...] += recv[d - 1].astype(F32)
    square = jnp.sum(state[...] * state[...], axis=1, keepdims=True)
    sums[...] = jnp.broadcast_to(square, (rows, 128))
    for d in range(1, n):
        to_group(d).start()
    grand = sums[...]
    for d in range(1, n):
        to_group(d).wait_recv()
        grand = grand + others[d - 1]
    weight = lax.rsqrt(grand / (share * n) + 1e-05) * guidance_ref[...]
    sums_now = state[...] * weight[:, :1]
    mixed = sums_now[:mine]
    for v in range(1, n):
        mixed = mixed + sums_now[v * mine : (v + 1) * mine]
    out_ref[tp, :mine, :] = (mixed * gain_ref[...]).astype(BF16)
    for d in range(1, chips):
        block_out(d, tp).start()
    pass_on(0, tp).start()
    for d in range(1, chips):
        owner = 2 * lax.rem(chip + chips - d, chips) + core
        block_out(d, owner).wait_recv()
        pass_on(d, owner).start()
    for d in range(chips):
        owner = 2 * lax.rem(chip + chips - d, chips) + 1 - core
        pass_on(d, owner).wait_recv()
    for d in range(chips):
        to_pair(d).wait_send()
        pass_on(d, tp).wait_send()
        if d:
            to_chip(d).wait_send()
            block_out(d, tp).wait_send()
    for d in range(1, n):
        to_group(d).wait_send()


def middle(n, m, branch, tokens, gain, guidance):
    _, rows, share = branch.shape
    chips = m // 2
    held = max(rows // n, 16)
    dma = pltpu.SemaphoreType.DMA
    vmem = pl.BlockSpec(memory_space=pltpu.VMEM)
    return pl.pallas_call(
        functools.partial(mid_kernel, n, m),
        out_shape=jax.ShapeDtypeStruct((m, held, share), BF16),
        in_specs=[vmem] * 4,
        out_specs=vmem,
        scratch_shapes=[
            pltpu.VMEM((chips, rows, share), BF16),
            pltpu.VMEM((chips - 1, rows, share), BF16),
            pltpu.VMEM((chips - 1, rows, share), BF16),
            pltpu.VMEM((rows, share), F32),
            pltpu.VMEM((rows, 128), F32),
            pltpu.VMEM((n - 1, rows, 128), F32),
            dma((2, chips)),
            dma((chips - 1,)),
            dma((chips - 1,)),
            dma((n - 1,)),
            dma((n - 1,)),
            dma((chips - 1,)),
            dma((chips - 1,)),
            dma((2, chips)),
        ],
        compiler_params=pltpu.CompilerParams(
            collective_id=2, has_side_effects=True, vmem_limit_bytes=40 * 1024 * 1024
        ),
        name="middle",
    )(branch, tokens, gain, guidance)


def local(tokens, gate_weight, up_weight, down_weight, norm_gain, unembed, guidance, logit_bias):
    variants = lax.axis_size("prompt")
    shards = lax.axis_size("tensor")
    rows = tokens.shape[1]
    share = gate_weight.shape[0]
    spread = lax.all_to_all(tokens, "prompt", split_axis=2, concat_axis=0, tiled=True)
    partial_branch = ffn(variants, spread, gate_weight, up_weight, down_weight)
    mine = rows // shards

    def by_owner(x):
        x = x.reshape(variants, shards, mine, share).swapaxes(0, 1)
        return x.reshape(shards, variants * mine, share)

    weight = jnp.broadcast_to(jnp.repeat(guidance, mine)[:, None], (variants * mine, 128))
    mixed = middle(
        variants, shards, by_owner(partial_branch), by_owner(spread), norm_gain[None, :], weight
    )
    mixed = mixed[:, :mine].reshape(rows, share)
    return head(variants, shards, mixed, unembed, logit_bias)


def solution(mesh):
    return jax.shard_map(
        local,
        mesh=mesh,
        in_specs=(
            P("prompt", None, None),
            P("prompt", "tensor"),
            P("prompt", "tensor"),
            P("tensor", "prompt"),
            P("prompt"),
            P("prompt", "tensor"),
            P(),
            P("prompt", "tensor"),
        ),
        out_specs=P("prompt", "tensor"),
        check_vma=False,
    )
```

profile of v0, /device:TPU:1, one launch (start us, length us, event | category | flops | bytes accessed | tf_op | source)
XLA Modules:
  0.0 312.3 jit_solution(18188190210180383139)
XLA Ops:
  0.0 9.5 %copy.15 = bf16[1,128,8192]{1,0,2:T(2,128)(2,1)} copy(bf16[1,128,8192]{2,1,0:T(8,128)(2,1)} %param.8) | data formatting | bytes 4194304 | tf_op args[0]
  9.5 0.5 broadcast
  10.0 45.2 %reduce = bf16[8192,128]{1,0:T(8,128)(2,1)S(1)} reduce(bf16[8192,1,128]{2,1,0:T(2,128)(2,1)} %bitcast.23, bf16[]{:T(256)} %broadcast), dimensions={1}, to_apply=%bitcast.15.reduce_sub_computation | reduce | bytes 4194306
  55.2 2.1 reshape.22
  57.3 0.0 copy-start.3
  57.3 4.4 %all-to-all-start = ((bf16[4,2,131072]{2,1,0:T(2,128)(2,1)}), bf16[4,2,131072]{2,1,0:T(2,128)(2,1)S(1)}, u32[]{:S(2)}, u32[]{:S(2)}) async-start(bf16[4,2,131072]{2,1,0:T(2,128)(2,1)} %reshape.22), calls=%async_computation | async-start | bytes 4194304 | tf_op jit(solution)/shard_map/all_to_all | solution.py:440
  61.7 0.0 copy-done.3
  61.7 0.1 broadcast_in_dim.14
  61.8 0.1 broadcast_in_dim.15
  61.8 24.2 %all-to-all-done = bf16[4,2,131072]{2,1,0:T(2,128)(2,1)S(1)} async-done(((bf16[4,2,131072]{2,1,0:T(2,128)(2,1)}), bf16[4,2,131072]{2,1,0:T(2,128)(2,1)S(1)}, u32[]{:S(2)}, u32[]{:S(2)}) %all-to-all-start) | async-done | bytes 2097184 | tf_op jit(solution)/shard_map/all_to_all | solution.py:440
  86.0 3.3 %reshape.23 = bf16[8192,1,128]{2,1,0:T(2,128)(2,1)} reshape(bf16[4,2,131072]{2,1,0:T(2,128)(2,1)S(1)} %all-to-all-done) | data formatting | bytes 4194304
  89.4 2.5 copy.19
  91.8 2.7 copy.16
  94.5 127.1 %ffn.1 = bf16[512,2048]{1,0:T(8,128)(2,1)} custom-call(bf16[4,128,2048]{2,1,0:T(8,128)(2,1)} %bitcast.21, bf16[2048,3584]{1,0:T(8,128)(2,1)} %gate_hbm.1, bf16[2048,3584]{1,0:T(8,128)(2,1)} %up_hbm.1, bf16[3584,2048]{1,0:T(8,128)(2,1)} %down_hbm.1), custom_call_target="tpu_custom_call" | custom-call | tf_op jit(solution)/shard_map/ffn/pallas_call | solution.py:141
  221.6 0.0 copy-start.2
  221.7 2.0 copy.17
  223.6 0.2 copy-done.2
  223.9 0.0 copy-start.1
  223.9 0.1 copy.18
  224.0 0.1 broadcast_in_dim.16.guidance_ref
  224.1 0.5 copy-done.1
  224.6 0.0 copy-start
  224.6 41.3 %middle.1 = bf16[8,16,2048]{2,1,0:T(8,128)(2,1)S(1)} custom-call(bf16[8,64,2048]{2,1,0:T(8,128)(2,1)S(1)} %bitcast.17, bf16[8,64,2048]{2,1,0:T(8,128)(2,1)S(1)} %bitcast.18, f32[1,2048]{1,0:T(1,128)S(1)} %bitcast.20, f32[64,128]{1,0:T(8,128)S(1)} %broadcast_in_dim.16.guidance_ref), custom_call_target="tpu_custom_call" | custom-call | tf_op jit(solution)/shard_map/middle/pallas_call | solution.py:407
  265.9 0.0 copy-done
  265.9 45.3 %head.1 = f32[32,10752]{1,0:T(8,128)S(1)} custom-call(bf16[128,2048]{1,0:T(8,128)(2,1)S(1)} %bitcast.19, bf16[2048,10752]{1,0:T(8,128)(2,1)} %unembed_hbm.1, f32[32,10752]{1,0:T(8,128)S(1)} %copy-done), custom_call_target="tpu_custom_call" | custom-call | tf_op jit(solution)/shard_map/head/pallas_call | solution.py:268
  311.2 1.1 copy.21
Async XLA Ops:
  57.3 4.4 %copy-start.3 = (f32[4]{0:T(128)S(1)}, f32[4]{0:T(128)}, u32[]{:S(2)}) copy-start(f32[4]{0:T(128)} %param.14) | copy-start | bytes 52
  57.3 28.7 %all-to-all-start = ((bf16[4,2,131072]{2,1,0:T(2,128)(2,1)}), bf16[4,2,131072]{2,1,0:T(2,128)(2,1)S(1)}, u32[]{:S(2)}, u32[]{:S(2)}) async-start(bf16[4,2,131072]{2,1,0:T(2,128)(2,1)} %reshape.22), calls=%async_computation | async-start | bytes 4194304 | tf_op jit(solution)/shard_map/all_to_all | solution.py:440
  221.6 2.2 copy-start.2
  223.9 0.7 copy-start.1
  224.6 41.3 %copy-start = (f32[32,10752]{1,0:T(8,128)S(1)}, f32[32,10752]{1,0:T(8,128)}, u32[]{:S(2)}) copy-start(f32[32,10752]{1,0:T(8,128)} %bias_ref.1) | copy-start | bytes 4128772
where the time goes:
time: 313 us; the launch traced here: 312 us
  Pallas kernels  214 us (68%)
  other arithmetic  45.2 us (14%)
  local copies, waits for them, and re-layouts  24.7 us (8%)
  waiting for transfers between devices  24.2 us (8%)
  starting transfers between devices  4.4 us (1%)
    pallas_call x1, Pallas kernels, ffn(): pl.pallas_call(functools.partial(ffn_kernel, n), out_shape=jax.ShapeDtype...  127 us
    pallas_call x1, Pallas kernels, head(): pl.pallas_call(functools.partial(head_kernel, n, m), out_shape=jax.ShapeD...  45.3 us
    unnamed x1, other arithmetic  45.2 us
    pallas_call x1, Pallas kernels, middle(): pl.pallas_call(functools.partial(mid_kernel, n, m), out_shape=jax.ShapeDt...  41.3 us
    all_to_all x1, waiting for transfers between devices, local(): lax.all_to_all(tokens, 'prompt', split_axis=2, concat_axis=0, tiled=True)  24.2 us
    unnamed x14, local copies, waits for them, and re-layouts  19.7 us
  transfers between devices with their start and end apart: 1, of which 1 were waited for; matrix products, arithmetic and copies ran while one was open for 0% of the time, Pallas kernels for 0%

commit v1 on v0

--- a/solution.py
+++ b/solution.py
@@ -167,14 +167,247 @@
     )(x, gate_weight, up_weight, down_weight)
 
 
+def flip(me, mask):
+    low, high = lax.rem(me, 2), me // 2
+    if mask == 1:
+        return me + 1 - 2 * low
+    if mask == 2:
+        return me + 2 - 4 * high
+    return 3 - me
+
+
+def partners(me, k):
+    one, two = flip(me, 1), flip(me, 2)
+    odd = lax.rem(k, 2)
+    return one + odd * (two - one), two + odd * (one - two)
+
+
+def ffn4_kernel(
+    tokens_hbm, gate_hbm, up_hbm, down_hbm, out_ref, x_ref,
+    wg, wu, wd, part, send, recv, send2, recv2, own, hid, acc,
+    w_sem, d_sem, t_sem, ts_sem, tr_sem, tf_sem,
+    as_sem, ar_sem, bs_sem, br_sem, hs_sem, hr_sem,
+):
+    n = 4
+    me = lax.axis_index("prompt")
+    tp = lax.axis_index("tensor")
+    core = lax.rem(tp, 2)
+    other_core = tp + 1 - 2 * core
+    rows, share = x_ref.shape[1:]
+    half = rows // 2
+    steps, chunk = hid.shape[0], hid.shape[3]
+    diagonal = flip(me, 3)
+
+    def weights(k, slot):
+        at = pl.ds(pl.multiple_of(k * chunk, chunk), chunk)
+        return (
+            pltpu.make_async_copy(gate_hbm.at[:, at], wg.at[slot], w_sem.at[slot, 0]),
+            pltpu.make_async_copy(up_hbm.at[:, at], wu.at[slot], w_sem.at[slot, 1]),
+        )
+
+    def down(k, slot):
+        at = pl.ds(pl.multiple_of(k * chunk, chunk), chunk)
+        return pltpu.make_async_copy(down_hbm.at[at, :], wd.at[slot], d_sem.at[slot])
+
+    def columns(q):
+        return pl.ds(pl.multiple_of(q * share, share), share)
+
+    my_half = pl.ds(pl.multiple_of(core * half, half), half)
+    other_half = pl.ds(pl.multiple_of((1 - core) * half, half), half)
+
+    def tokens_to(d):
+        q = lax.rem(me + d, n)
+        return pltpu.make_async_remote_copy(
+            src_ref=tokens_hbm.at[my_half, columns(q)], dst_ref=x_ref.at[me, my_half],
+            send_sem=ts_sem.at[d - 1], recv_sem=tr_sem.at[d - 1],
+            device_id={"prompt": q}, device_id_type=MESH,
+        )
+
+    def tokens_over(d, at):
+        v = lax.rem(me + n - d, n)
+        return pltpu.make_async_remote_copy(
+            src_ref=x_ref.at[v, at], dst_ref=x_ref.at[v, at],
+            send_sem=tf_sem.at[0, d - 1], recv_sem=tf_sem.at[1, d - 1],
+            device_id={"tensor": other_core}, device_id_type=MESH,
+        )
+
+    def to_first(k):
+        return pltpu.make_async_remote_copy(
+            src_ref=send.at[k], dst_ref=recv.at[k],
+            send_sem=as_sem.at[k], recv_sem=ar_sem.at[k],
+            device_id={"prompt": partners(me, k)[0]}, device_id_type=MESH,
+        )
+
+    def to_second(k):
+        return pltpu.make_async_remote_copy(
+            src_ref=send2.at[k], dst_ref=recv2.at[k],
+            send_sem=bs_sem.at[k], recv_sem=br_sem.at[k],
+            device_id={"prompt": partners(me, k)[1]}, device_id_type=MESH,
+        )
+
+    def hid_to(k, which, owner, to):
+        return pltpu.make_async_remote_copy(
+            src_ref=hid.at[k, owner], dst_ref=hid.at[k, owner],
+            send_sem=hs_sem.at[k, which], recv_sem=hr_sem.at[k, which],
+            device_id={"prompt": to}, device_id_type=MESH,
+        )
+
+    for copy in weights(0, 0):
+        copy.start()
+    down(0, 0).start()
+    keep = pltpu.make_async_copy(tokens_hbm.at[:, columns(me)], x_ref.at[me], t_sem.at[0])
+    keep.start()
+    barrier = pltpu.get_barrier_semaphore()
+    for d in range(1, n):
+        pl.semaphore_signal(barrier, inc=1, device_id={"prompt": lax.rem(me + d, n)}, device_id_type=MESH)
+    pl.semaphore_signal(barrier, inc=1, device_id={"tensor": other_core}, device_id_type=MESH)
+    pl.semaphore_wait(barrier, n)
+    for d in range(1, n):
+        tokens_to(d).start()
+    for d in range(1, n):
+        tokens_to(d).wait_recv()
+        tokens_over(d, my_half).start()
+    keep.wait()
+    for d in range(1, n):
+        tokens_over(d, other_half).wait_recv()
+
+    @pl.loop(0, steps)
+    def _(k):
+        slot = lax.rem(k, 2)
+        for copy in weights(k, slot):
+            copy.wait()
+
+        @pl.when(k + 1 < steps)
+        def _():
+            for copy in weights(k + 1, 1 - slot):
+                copy.start()
+
+        x = x_ref[...].reshape(n * rows, share)
+        part[:, :, :chunk] = jnp.dot(x, wg[slot], preferred_element_type=F32).reshape(n, rows, chunk)
+        part[:, :, chunk:] = jnp.dot(x, wu[slot], preferred_element_type=F32).reshape(n, rows, chunk)
+        first, second = partners(me, k)
+        send[k, 0] = part[diagonal].astype(BF16)
+        send[k, 1] = part[first].astype(BF16)
+        to_first(k).start()
+        own[k, 0] = part[second]
+        own[k, 1] = part[me]
+
+    @pl.loop(0, steps)
+    def _(k):
+        to_first(k).wait_recv()
+        send2[k] = (own[k, 0] + recv[k, 0].astype(F32)).astype(BF16)
+        to_second(k).start()
+
+    @pl.loop(0, steps)
+    def _(k):
+        first, second = partners(me, k)
+        to_second(k).wait_recv()
+        total = own[k, 1] + recv[k, 1].astype(F32) + recv2[k].astype(F32)
+        gate = total[:, :chunk]
+        hid[k, me] = (gate / (1.0 + jnp.exp(-gate)) * total[:, chunk:]).astype(BF16)
+        hid_to(k, 0, me, first).start()
+        hid_to(k, 1, me, second).start()
+
+    @pl.loop(0, steps)
+    def _(k):
+        first, second = partners(me, k)
+        hid_to(k, 0, first, first).wait_recv()
+        hid_to(k, 2, first, second).start()
+
+    acc[...] = jnp.zeros_like(acc)
+    tile = step_of(share, 512)
+
+    @pl.loop(0, steps)
+    def _(k):
+        slot = lax.rem(k, 2)
+        first, second = partners(me, k)
+        down(k, slot).wait()
+
+        @pl.when(k + 1 < steps)
+        def _():
+            down(k + 1, 1 - slot).start()
+
+        hid_to(k, 1, second, second).wait_recv()
+        hid_to(k, 2, diagonal, second).wait_recv()
+        h = hid[k].reshape(n * rows, chunk)
+        for t in range(share // tile):
+            at = slice(t * tile, (t + 1) * tile)
+            acc[:, at] += jnp.dot(h, wd[slot, :, at], preferred_element_type=F32)
+
+    out_ref[...] = acc[...].astype(BF16)
+
+    for d in range(1, n):
+        tokens_to(d).wait_send()
+        tokens_over(d, my_half).wait_send()
+
+    @pl.loop(0, steps)
+    def _(k):
+        first, second = partners(me, k)
+        to_first(k).wait_send()
+        to_second(k).wait_send()
+        hid_to(k, 0, me, first).wait_send()
+        hid_to(k, 1, me, second).wait_send()
+        hid_to(k, 2, first, second).wait_send()
+
+
+def ffn4(tokens, gate_weight, up_weight, down_weight):
+    n = 4
+    rows = tokens.shape[0]
+    share, width = gate_weight.shape
+    chunk = step_of(width, 256)
+    steps = width // chunk
+    dma = pltpu.SemaphoreType.DMA
+    hbm = pl.BlockSpec(memory_space=pl.ANY)
+    vmem = pl.BlockSpec(memory_space=pltpu.VMEM)
+    return pl.pallas_call(
+        ffn4_kernel,
+        out_shape=(
+            jax.ShapeDtypeStruct((n * rows, share), BF16),
+            jax.ShapeDtypeStruct((n, rows, share), BF16),
+        ),
+        in_specs=[hbm, hbm, hbm, hbm],
+        out_specs=(vmem, vmem),
+        scratch_shapes=[
+            pltpu.VMEM((2, share, chunk), BF16),
+            pltpu.VMEM((2, share, chunk), BF16),
+            pltpu.VMEM((2, chunk, share), BF16),
+            pltpu.VMEM((n, rows, 2 * chunk), F32),
+            pltpu.VMEM((steps, 2, rows, 2 * chunk), BF16),
+            pltpu.VMEM((steps, 2, rows, 2 * chunk), BF16),
+            pltpu.VMEM((steps, rows, 2 * chunk), BF16),
+            pltpu.VMEM((steps, rows, 2 * chunk), BF16),
+            pltpu.VMEM((steps, 2, rows, 2 * chunk), F32),
+            pltpu.VMEM((steps, n, rows, chunk), BF16),
+            pltpu.VMEM((n * rows, share), F32),
+            dma((2, 2)),
+            dma((2,)),
+            dma((1,)),
+            dma((n - 1,)),
+            dma((n - 1,)),
+            dma((2, n - 1)),
+            dma((steps,)),
+            dma((steps,)),
+            dma((steps,)),
+            dma((steps,)),
+            dma((steps, 3)),
+            dma((steps, 3)),
+        ],
+        compiler_params=pltpu.CompilerParams(
+            collective_id=0, has_side_effects=True, vmem_limit_bytes=56 * 1024 * 1024
+        ),
+        name="ffn4",
+    )(tokens, gate_weight, up_weight, down_weight)
+
+
 def head_kernel(
     n, m, x_ref, unembed_hbm, bias_ref, out_ref,
-    w, send, recv, own, mine, stats,
-    w_sem, ps_sem, pr_sem, ss_sem, sr_sem,
+    w, send, recv, send2, recv2, keep, own, mine, stats,
+    w_sem, ps_sem, pr_sem, bs_sem, br_sem, ss_sem, sr_sem,
 ):
     me = lax.axis_index("prompt")
     tp = lax.axis_index("tensor")
     steps, _, rows, chunk = send.shape
+    paired = n == 4
     slots = w.shape[0]
 
     def columns(k):
@@ -192,6 +425,20 @@
             device_id={"prompt": q}, device_id_type=MESH,
         )
 
+    def to_first(k):
+        return pltpu.make_async_remote_copy(
+            src_ref=send.at[k], dst_ref=recv.at[k],
+            send_sem=ps_sem.at[k, 0], recv_sem=pr_sem.at[k, 0],
+            device_id={"prompt": partners(me, k)[0]}, device_id_type=MESH,
+        )
+
+    def to_second(k):
+        return pltpu.make_async_remote_copy(
+            src_ref=send2.at[k], dst_ref=recv2.at[k],
+            send_sem=bs_sem.at[k], recv_sem=br_sem.at[k],
+            device_id={"prompt": partners(me, k)[1]}, device_id_type=MESH,
+        )
+
     def send_stats(d):
         return pltpu.make_async_remote_copy(
             src_ref=mine, dst_ref=stats.at[d - 1],
@@ -213,17 +460,36 @@
 
         product = jnp.dot(x_ref[...], w[lax.rem(k, slots)], preferred_element_type=F32)
         own[...] = product.reshape(n, rows, chunk)
-        send[k] = own[...].astype(BF16)
         out_ref[:, columns(k)] = own[me]
-        for d in range(1, n):
-            send_part(k, d).start()
+        if paired:
+            first, second = partners(me, k)
+            send[k, 0] = own[flip(me, 3)].astype(BF16)
+            send[k, 1] = own[first].astype(BF16)
+            keep[k] = own[second]
+            to_first(k).start()
+        else:
+            send[k] = own[...].astype(BF16)
+            for d in range(1, n):
+                send_part(k, d).start()
+
+    if paired:
+
+        @pl.loop(0, steps)
+        def _(k):
+            to_first(k).wait_recv()
+            send2[k] = (keep[k] + recv[k, 0].astype(F32)).astype(BF16)
+            to_second(k).start()
 
     def gather(k, top):
-        for d in range(1, n):
-            send_part(k, d).wait_recv()
         total = out_ref[:, columns(k)]
-        for d in range(1, n):
-            total = total + recv[k, d - 1].astype(F32)
+        if paired:
+            to_second(k).wait_recv()
+            total = total + recv[k, 1].astype(F32) + recv2[k].astype(F32)
+        else:
+            for d in range(1, n):
+                send_part(k, d).wait_recv()
+            for d in range(1, n):
+                total = total + recv[k, d - 1].astype(F32)
         total = total + bias_ref[:, columns(k)]
         out_ref[:, columns(k)] = total
         return jnp.maximum(top, jnp.max(total, axis=1, keepdims=True))
@@ -250,8 +516,12 @@
     @pl.loop(0, steps)
     def _(k):
         out_ref[:, columns(k)] = out_ref[:, columns(k)] - shift
-        for d in range(1, n):
-            send_part(k, d).wait_send()
+        if paired:
+            to_first(k).wait_send()
+            to_second(k).wait_send()
+        else:
+            for d in range(1, n):
+                send_part(k, d).wait_send()
 
     for d in range(1, m):
         send_stats(d).wait_send()
@@ -262,6 +532,7 @@
     rows = mixed.shape[0] // n
     chunk = step_of(width, 512)
     steps = width // chunk
+    sent, got, extra = (2, 2, steps) if n == 4 else (n, n - 1, 1)
     dma = pltpu.SemaphoreType.DMA
     hbm = pl.BlockSpec(memory_space=pl.ANY)
     vmem = pl.BlockSpec(memory_space=pltpu.VMEM)
@@ -272,14 +543,19 @@
         out_specs=vmem,
         scratch_shapes=[
             pltpu.VMEM((4, share, chunk), BF16),
-            pltpu.VMEM((steps, n, rows, chunk), BF16),
-            pltpu.VMEM((steps, n - 1, rows, chunk), BF16),
+            pltpu.VMEM((steps, sent, rows, chunk), BF16),
+            pltpu.VMEM((steps, got, rows, chunk), BF16),
+            pltpu.VMEM((extra, rows, chunk), BF16),
+            pltpu.VMEM((extra, rows, chunk), BF16),
+            pltpu.VMEM((extra, rows, chunk), F32),
             pltpu.VMEM((n, rows, chunk), F32),
             pltpu.VMEM((2, rows, 128), F32),
             pltpu.VMEM((m - 1, 2, rows, 128), F32),
             dma((4,)),
             dma((steps, n - 1)),
             dma((steps, n - 1)),
+            dma((extra,)),
+            dma((extra,)),
             dma((m - 1,)),
             dma((m - 1,)),
         ],
@@ -437,8 +713,11 @@
     shards = lax.axis_size("tensor")
     rows = tokens.shape[1]
     share = gate_weight.shape[0]
-    spread = lax.all_to_all(tokens, "prompt", split_axis=2, concat_axis=0, tiled=True)
-    partial_branch = ffn(variants, spread, gate_weight, up_weight, down_weight)
+    if variants == 4:
+        partial_branch, spread = ffn4(tokens[0], gate_weight, up_weight, down_weight)
+    else:
+        spread = lax.all_to_all(tokens, "prompt", split_axis=2, concat_axis=0, tiled=True)
+        partial_branch = ffn(variants, spread, gate_weight, up_weight, down_weight)
     mine = rows // shards
 
     def by_owner(x):

time: 313 us -> 209 us (0.67)
  other arithmetic: 45.2 us -> 0 us
  waiting for transfers between devices: 24.2 us -> 0 us
  local copies, waits for them, and re-layouts: 24.7 us -> 6.61 us
  Pallas kernels: 214 us -> 201 us
  starting transfers between devices: 4.4 us -> 0 us
    unnamed x1 -> x0, other arithmetic: 45.2 us -> none
    all_to_all x1 -> x0, waiting for transfers between devices: 24.2 us -> none  [local(): lax.all_to_all(tokens, 'prompt', split_axis=2, concat_axis=0, tiled=True)]
    unnamed x14 -> x11, local copies, waits for them, and re-layouts: 19.7 us -> 3.03 us
    pallas_call x1, Pallas kernels: 45.3 us -> 39.6 us  [head(): pl.pallas_call(functools.partial(head_kernel, n, m), out_shape=jax.ShapeD...]
    all_to_all x1 -> x0, starting transfers between devices: 4.4 us -> none  [local(): lax.all_to_all(tokens, 'prompt', split_axis=2, concat_axis=0, tiled=True)]
    pallas_call x1, Pallas kernels: 127 us -> 123 us  [ffn4(): pl.pallas_call(ffn4_kernel, out_shape=(jax.ShapeDtypeStruct((n * rows, sh...]
  transfers between devices with their start and end apart: 1 -> 0, of which waited for: 1 -> 0; matrix products, arithmetic and copies ran while one was open for 0% -> 0% of each run, Pallas kernels for 0% -> 0%
where the time goes in v1:
time: 209 us; the launch traced here: 208 us
  Pallas kernels  201 us (96%)
  local copies, waits for them, and re-layouts  6.61 us (3%)
    pallas_call x1, Pallas kernels, ffn4(): pl.pallas_call(ffn4_kernel, out_shape=(jax.ShapeDtypeStruct((n * rows, sh...  123 us
    pallas_call x1, Pallas kernels, head(): pl.pallas_call(functools.partial(head_kernel, n, m), out_shape=jax.ShapeD...  39.6 us
    pallas_call x1, Pallas kernels, middle(): pl.pallas_call(functools.partial(mid_kernel, n, m), out_shape=jax.ShapeDt...  38.5 us

profile of v1, /device:TPU:1, one launch (start us, length us, event | category | flops | bytes accessed | tf_op | source)
XLA Modules:
  0.0 207.5 jit_solution(18117228473652161415)
XLA Ops:
  0.0 122.8 %ffn4.1 = (bf16[512,2048]{1,0:T(8,128)(2,1)}, bf16[4,128,2048]{2,1,0:T(8,128)(2,1)}) custom-call(bf16[128,8192]{1,0:T(8,128)(2,1)} %bitcast.15, bf16[2048,3584]{1,0:T(8,128)(2,1)} %gate_hbm.1, bf16[2048,3584]{1,0:T(8,128)(2,1)} %up_hbm.1, bf16[3584,2048]{1,0:T(8,128)(2,1)} %down_hbm.1), custom_call_target="tpu_custom_call" | custom-call | tf_op jit(solution)/shard_map/ffn4/pallas_call | solution.py:362
  122.8 0.0 copy-start.3
  122.8 1.9 copy.9
  124.7 0.3 copy-done.3
  125.0 0.0 copy-start.4
  125.0 0.0 copy-start.2
  125.0 1.5 copy.10
  126.5 0.0 copy-done.4
  126.5 0.1 broadcast_in_dim.14
  126.6 0.1 broadcast_in_dim.15
  126.6 0.1 broadcast_in_dim.16.guidance_ref
  126.7 0.0 copy-done.2
  126.7 0.0 copy-start
  126.7 1.6 copy-done
  128.3 0.0 copy-start.1
  128.3 38.5 %middle.1 = bf16[8,16,2048]{2,1,0:T(8,128)(2,1)S(1)} custom-call(bf16[8,64,2048]{2,1,0:T(8,128)(2,1)S(1)} %bitcast.11, bf16[8,64,2048]{2,1,0:T(8,128)(2,1)S(1)} %bitcast.12, f32[1,2048]{1,0:T(1,128)S(1)} %bitcast.14, f32[64,128]{1,0:T(8,128)S(1)} %broadcast_in_dim.16.guidance_ref), custom_call_target="tpu_custom_call" | custom-call | tf_op jit(solution)/shard_map/middle/pallas_call | solution.py:683
  166.9 0.0 copy-done.1
  166.9 39.6 %head.1 = f32[32,10752]{1,0:T(8,128)S(1)} custom-call(bf16[128,2048]{1,0:T(8,128)(2,1)S(1)} %bitcast.13, bf16[2048,10752]{1,0:T(8,128)(2,1)} %unembed_hbm.1, f32[32,10752]{1,0:T(8,128)S(1)} %copy-done.1), custom_call_target="tpu_custom_call" | custom-call | tf_op jit(solution)/shard_map/head/pallas_call | solution.py:539
  206.4 1.1 copy.12
Async XLA Ops:
  122.8 2.2 %copy-start.3 = (bf16[4,128,2048]{2,1,0:T(8,128)(2,1)S(1)}, bf16[4,128,2048]{2,1,0:T(8,128)(2,1)}, u32[]{:S(2)}) copy-start(bf16[4,128,2048]{2,1,0:T(8,128)(2,1)} %get-tuple-element.8) | copy-start | bytes 6291460
  125.0 1.5 copy-start.4
  125.0 1.7 copy-start.2
  126.7 1.6 copy-start
  128.3 38.6 %copy-start.1 = (f32[32,10752]{1,0:T(8,128)S(1)}, f32[32,10752]{1,0:T(8,128)}, u32[]{:S(2)}) copy-start(f32[32,10752]{1,0:T(8,128)} %bias_ref.1) | copy-start | bytes 4128772

commit v2 on v1

--- a/solution.py
+++ b/solution.py
@@ -183,8 +183,8 @@
 
 
 def ffn4_kernel(
-    tokens_hbm, gate_hbm, up_hbm, down_hbm, out_ref, x_ref,
-    wg, wu, wd, part, send, recv, send2, recv2, own, hid, acc,
+    tokens_hbm, gate_hbm, up_hbm, down_hbm, out_ref, mine_ref,
+    x_ref, wg, wu, wd, part, send, recv, send2, recv2, own, hid, acc,
     w_sem, d_sem, t_sem, ts_sem, tr_sem, tf_sem,
     as_sem, ar_sem, bs_sem, br_sem, hs_sem, hr_sem,
 ):
@@ -334,7 +334,14 @@
             at = slice(t * tile, (t + 1) * tile)
             acc[:, at] += jnp.dot(h, wd[slot, :, at], preferred_element_type=F32)
 
-    out_ref[...] = acc[...].astype(BF16)
+    mine = mine_ref.shape[0] // n
+    my_rows = pl.ds(pl.multiple_of(tp * mine, mine), mine)
+    for v in range(n):
+        at = slice(v * mine, (v + 1) * mine)
+        mine_ref[at, :] = x_ref[v, my_rows, :]
+        for j in range(rows // mine):
+            row = v * rows + j * mine
+            out_ref[j, at, :] = acc[row : row + mine, :].astype(BF16)
 
     for d in range(1, n):
         tokens_to(d).wait_send()
@@ -350,7 +357,7 @@
         hid_to(k, 2, first, second).wait_send()
 
 
-def ffn4(tokens, gate_weight, up_weight, down_weight):
+def ffn4(m, tokens, gate_weight, up_weight, down_weight):
     n = 4
     rows = tokens.shape[0]
     share, width = gate_weight.shape
@@ -362,12 +369,13 @@
     return pl.pallas_call(
         ffn4_kernel,
         out_shape=(
-            jax.ShapeDtypeStruct((n * rows, share), BF16),
-            jax.ShapeDtypeStruct((n, rows, share), BF16),
+            jax.ShapeDtypeStruct((m, n * rows // m, share), BF16),
+            jax.ShapeDtypeStruct((n * rows // m, share), BF16),
         ),
         in_specs=[hbm, hbm, hbm, hbm],
         out_specs=(vmem, vmem),
         scratch_shapes=[
+            pltpu.VMEM((n, rows, share), BF16),
             pltpu.VMEM((2, share, chunk), BF16),
             pltpu.VMEM((2, share, chunk), BF16),
             pltpu.VMEM((2, chunk, share), BF16),
@@ -450,8 +458,7 @@
         weights(k).start()
     greet([("prompt", n), ("tensor", m)])
 
-    @pl.loop(0, steps)
-    def _(k):
+    def multiply(k):
         weights(k).wait()
 
         @pl.when(k + slots - 1 < steps)
@@ -472,13 +479,26 @@
             for d in range(1, n):
                 send_part(k, d).start()
 
-    if paired:
-
-        @pl.loop(0, steps)
-        def _(k):
-            to_first(k).wait_recv()
-            send2[k] = (keep[k] + recv[k, 0].astype(F32)).astype(BF16)
-            to_second(k).start()
+    def relay(k):
+        to_first(k).wait_recv()
+        send2[k] = (keep[k] + recv[k, 0].astype(F32)).astype(BF16)
+        to_second(k).start()
+
+    lag = min(3, steps) if paired else 0
+
+    @pl.loop(0, lag)
+    def _(k):
+        multiply(k)
+
+    @pl.loop(lag, steps)
+    def _(k):
+        multiply(k)
+        if paired:
+            relay(k - lag)
+
+    @pl.loop(steps - lag, steps)
+    def _(k):
+        relay(k)
 
     def gather(k, top):
         total = out_ref[:, columns(k)]
@@ -635,7 +655,7 @@
         to_chip(d).start()
     to_pair(chip).wait_recv()
     state[...] = (
-        tokens_ref[tp].astype(F32) + branch_ref[tp].astype(F32) + pair[chip].astype(F32)
+        tokens_ref[...].astype(F32) + branch_ref[tp].astype(F32) + pair[chip].astype(F32)
     )
     for d in range(1, chips):
         to_chip(d).wait_recv()
@@ -713,20 +733,21 @@
     shards = lax.axis_size("tensor")
     rows = tokens.shape[1]
     share = gate_weight.shape[0]
+    mine = rows // shards
     if variants == 4:
-        partial_branch, spread = ffn4(tokens[0], gate_weight, up_weight, down_weight)
+        branch, own = ffn4(shards, tokens[0], gate_weight, up_weight, down_weight)
     else:
+
+        def by_owner(x):
+            x = x.reshape(variants, shards, mine, share).swapaxes(0, 1)
+            return x.reshape(shards, variants * mine, share)
+
         spread = lax.all_to_all(tokens, "prompt", split_axis=2, concat_axis=0, tiled=True)
-        partial_branch = ffn(variants, spread, gate_weight, up_weight, down_weight)
-    mine = rows // shards
-
-    def by_owner(x):
-        x = x.reshape(variants, shards, mine, share).swapaxes(0, 1)
-        return x.reshape(shards, variants * mine, share)
-
+        branch = by_owner(ffn(variants, spread, gate_weight, up_weight, down_weight))
+        own = lax.dynamic_index_in_dim(by_owner(spread), lax.axis_index("tensor"), 0, keepdims=False)
     weight = jnp.broadcast_to(jnp.repeat(guidance, mine)[:, None], (variants * mine, 128))
     mixed = middle(
-        variants, shards, by_owner(partial_branch), by_owner(spread), norm_gain[None, :], weight
+        variants, shards, branch, own, norm_gain[None, :], weight
     )
     mixed = mixed[:, :mine].reshape(rows, share)
     return head(variants, shards, mixed, unembed, logit_bias)

time: 209 us -> 208 us (level)
  local copies, waits for them, and re-layouts: 6.61 us -> 4.5 us
    reshape x2 -> x0, local copies, waits for them, and re-layouts: 3.35 us -> none  [by_owner(): x = x.reshape(variants, shards, mine, share).swapaxes(0, 1)]
where the time goes in v2:
time: 208 us; the launch traced here: 207 us
  Pallas kernels  202 us (97%)
  local copies, waits for them, and re-layouts  4.5 us (2%)
    pallas_call x1, Pallas kernels, ffn4(): pl.pallas_call(ffn4_kernel, out_shape=(jax.ShapeDtypeStruct((m, n * rows...  122 us
    pallas_call x1, Pallas kernels, head(): pl.pallas_call(functools.partial(head_kernel, n, m), out_shape=jax.ShapeD...  41.6 us
    pallas_call x1, Pallas kernels, middle(): pl.pallas_call(functools.partial(mid_kernel, n, m), out_shape=jax.ShapeDt...  38.5 us

profile of v2, /device:TPU:1, one launch (start us, length us, event | category | flops | bytes accessed | tf_op | source)
XLA Modules:
  0.0 207.0 jit_solution(6828931912236240476)
XLA Ops:
  0.0 0.7 broadcast_in_dim.14
  0.7 0.1 broadcast_in_dim.15
  0.8 0.1 broadcast_in_dim.16.guidance_ref
  0.9 0.0 copy-start.3
  0.9 0.0 copy-start.1
  0.9 122.3 %ffn4.1 = (bf16[8,64,2048]{2,1,0:T(8,128)(2,1)}, bf16[64,2048]{1,0:T(8,128)(2,1)}) custom-call(bf16[128,8192]{1,0:T(8,128)(2,1)} %bitcast.5, bf16[2048,3584]{1,0:T(8,128)(2,1)} %gate_hbm.1, bf16[2048,3584]{1,0:T(8,128)(2,1)} %up_hbm.1, bf16[3584,2048]{1,0:T(8,128)(2,1)} %down_hbm.1), custom_call_target="tpu_custom_call" | custom-call | tf_op jit(solution)/shard_map/ffn4/pallas_call | solution.py:369
  123.2 0.0 copy-done.3
  123.2 0.0 copy-start
  123.2 1.6 copy-done
  124.8 0.0 copy-start.2
  124.8 0.9 copy-done.2
  125.8 38.5 %middle.1 = bf16[8,16,2048]{2,1,0:T(8,128)(2,1)S(1)} custom-call(bf16[8,64,2048]{2,1,0:T(8,128)(2,1)S(1)} %copy-done, bf16[64,2048]{1,0:T(8,128)(2,1)S(1)} %copy-done.2, f32[1,2048]{1,0:T(1,128)S(1)} %bitcast.4, f32[64,128]{1,0:T(8,128)S(1)} %broadcast_in_dim.16.guidance_ref), custom_call_target="tpu_custom_call" | custom-call | tf_op jit(solution)/shard_map/middle/pallas_call | solution.py:703
  164.3 0.0 copy-done.1
  164.3 41.6 %head.1 = f32[32,10752]{1,0:T(8,128)S(1)} custom-call(bf16[128,2048]{1,0:T(8,128)(2,1)S(1)} %bitcast.3, bf16[2048,10752]{1,0:T(8,128)(2,1)} %unembed_hbm.1, f32[32,10752]{1,0:T(8,128)S(1)} %copy-done.1), custom_call_target="tpu_custom_call" | custom-call | tf_op jit(solution)/shard_map/head/pallas_call | solution.py:559
  205.9 1.1 copy.10
Async XLA Ops:
  0.9 122.3 %copy-start.3 = (f32[2048]{0:T(1024)S(1)}, f32[2048]{0:T(1024)}, u32[]{:S(2)}) copy-start(f32[2048]{0:T(1024)} %param.12) | copy-start | bytes 24580
  0.9 163.4 %copy-start.1 = (f32[32,10752]{1,0:T(8,128)S(1)}, f32[32,10752]{1,0:T(8,128)}, u32[]{:S(2)}) copy-start(f32[32,10752]{1,0:T(8,128)} %bias_ref.1) | copy-start | bytes 4128772
  123.2 1.6 copy-start
  124.8 0.9 copy-start.2
